TPU v7x, 32 devices: a whole 2x2x4 slice. The times are simulated.
32 devices in a mesh: groups: 1, train: 16 (over z, y, x), tensor: 2 (over core).
Axes of the slice: x: 2, y: 2, z: 4, core: 2. Of those that a mesh axis runs over, the one named last changes fastest.
Arguments:
- activations: bfloat16 [4096, 28672], P(('groups', 'train'), 'tensor'), may hold values from -6 to 6
- out_grads: bfloat16 [4096, 8192], P(('groups', 'train'), 'tensor'), may hold values from -6 to 6
- basis_in: bfloat16 [256, 28672], P('train', 'tensor'), may hold values from -0.375 to 0.375
- basis_out: bfloat16 [256, 8192], P('train', 'tensor'), may hold values from -0.375 to 0.375
- eigen_in: float32 [28672], P('tensor'), may hold values from 1 to 100
- eigen_out: float32 [8192], P('tensor'), may hold values from 1 to 100
- query_in: bfloat16 [28672, 64], P('tensor'), may hold values from -0.03125 to 0.03125
- query_out: bfloat16 [8192, 64], P('tensor'), may hold values from -0.0625 to 0.0625
- response_ids: int32 [4096], P(('groups', 'train')), may hold values from 0 to 63, as said below
- lengths: int32 [64], P(('groups', 'train')), may hold values from 1 to 127, as said below
- pair_ids: int32 [32], P('groups'), may hold values from 0 to 31, each once
Outputs:
- token_scores: float32 [4096, 8], P(('groups', 'train'), 'tensor')
- pair_scores: float32 [32, 8], P(('groups', 'train'), 'tensor')
Inputs may be any that keep to these rules, and one draw needn't show every extreme that they name: `response_ids`: tokens come in pair slots of 128 in a row, slot k holding responses 2 k (the chosen, first) and 2 k + 1 (the rejected): the first lengths[2 k] tokens of slot k carry id 2 k, the others 2 k + 1. lengths[2 k] + lengths[2 k + 1] = 128 for every slot k. `pair_ids`: A permutation of the pairs.
All inputs are finite; a program needn't handle non-finite values.
Results may differ from a plain program's by a relative error of at most 0.0003.
Values may be sent and summed in bfloat16 or wider, within the bound.
A program may use at most 64 MiB of HBM per device.

v0:
```python
import jax
import jax.numpy as jnp
from jax import lax
from jax.sharding import PartitionSpec as P

BLOCK_IN = 256
BLOCK_OUT = 256
RANK = 8
QUERIES = 8


def apply_fn(token_rows, fetched):
    return jnp.einsum(
        "tnk,nkm->tm",
        token_rows,
        fetched,
        precision=lax.Precision.HIGHEST,
        preferred_element_type=jnp.float32,
    )


def fold_local(basis, eigen, query, blocks, block_order):
    own_rows = basis.shape[0]
    scaled = (query.astype(jnp.float32) / eigen[:, None]).reshape(
        blocks, block_order, query.shape[1]
    )
    basis_part = basis.astype(jnp.float32).reshape(own_rows, blocks, block_order)
    return jnp.einsum("knj,njm->nkm", basis_part, scaled, precision=lax.Precision.HIGHEST)


def shards(
    activations,
    out_grads,
    basis_in,
    basis_out,
    eigen_in,
    eigen_out,
    query_in,
    query_out,
    response_ids,
    lengths,
    pair_ids,
):
    tok_rows = activations.shape[0]
    hidden_cols = activations.shape[1]
    feature_cols = out_grads.shape[1]
    blocks_in = hidden_cols // BLOCK_IN
    blocks_out = feature_cols // BLOCK_OUT
    rows_in = activations.reshape(tok_rows, blocks_in, BLOCK_IN)
    rows_out = out_grads.reshape(tok_rows, blocks_out, BLOCK_OUT)
    folded_in = fold_local(basis_in, eigen_in, query_in, blocks_in, BLOCK_IN)
    folded_out = fold_local(basis_out, eigen_out, query_out, blocks_out, BLOCK_OUT)
    proj_in = apply_fn(rows_in, lax.all_gather(folded_in, "train", axis=1, tiled=True))
    proj_out = apply_fn(rows_out, lax.all_gather(folded_out, "train", axis=1, tiled=True))
    proj_in, proj_out = lax.psum((proj_in, proj_out), "tensor")
    scores = (proj_in * proj_out).reshape(tok_rows, QUERIES, RANK).sum(axis=2)
    per_device = QUERIES // lax.axis_size("tensor")
    scores = lax.dynamic_slice_in_dim(scores, lax.axis_index("tensor") * per_device, per_device, 1)
    resp_dev = lengths.shape[0]
    local_ids = response_ids - lax.axis_index("train") * resp_dev
    member = (local_ids[None, :] == jnp.arange(resp_dev, dtype=jnp.int32)[:, None]).astype(
        jnp.float32
    )
    resp_sums = jnp.dot(member, scores, precision=lax.Precision.HIGHEST)
    averages = resp_sums / lengths.astype(jnp.float32)[:, None]
    slot_values = averages[0::2] - averages[1::2]
    every_slot = lax.all_gather(slot_values, "train", axis=0, tiled=True)
    pair_dev = slot_values.shape[0]
    own_pairs = lax.axis_index("train") * pair_dev + jnp.arange(pair_dev, dtype=jnp.int32)
    selector = (pair_ids[None, :] == own_pairs[:, None]).astype(jnp.float32)
    pair_scores = jnp.dot(selector, every_slot, precision=lax.Precision.HIGHEST)
    return (scores, pair_scores)


def solution(mesh):
    return jax.shard_map(
        shards,
        mesh=mesh,
        in_specs=(
            P(("groups", "train"), "tensor"),
            P(("groups", "train"), "tensor"),
            P("train", "tensor"),
            P("train", "tensor"),
            P("tensor"),
            P("tensor"),
            P("tensor", None),
            P("tensor", None),
            P(("groups", "train")),
            P(("groups", "train")),
            P("groups"),
        ),
        out_specs=(P(("groups", "train"), "tensor"), P(("groups", "train"), "tensor")),
        check_vma=False,
    )
```

profile of v0, /device:TPU:0, one launch (start us, length us, event | category | flops | bytes accessed | tf_op | source)
XLA Modules:
  0.0 264.9 jit_solution(3484073163096825936)
XLA Ops:
  7.2 0.0 copy-start.1
  7.2 0.0 all-gather.6.cloned.1.call-start
  7.2 1.2 convert_divide_fusion.1
  8.5 0.0 copy-start.2
  8.5 2.2 convolution_bitcast_fusion
  10.7 0.0 all-gather.6.cloned.1.call-update
  10.7 0.0 all-gather.4.cloned.1.call-start
  10.8 0.0 copy-done.1
  10.8 1.1 convert_divide_fusion
  11.9 0.0 copy-start
  11.9 0.0 copy-done.2
  11.9 2.6 fusion.9
  14.5 0.0 all-gather.4.cloned.1.call-update
  14.6 0.0 all-reduce.3.cloned.1.call-start
  14.6 60.7 %all-gather.6.cloned.1.call-done = f32[16,256,64]{2,1,0:T(8,128)} async-done(((f32[16,16,64]{2,1,0:T(8,128)}), f32[16,256,64]{2,1,0:T(8,128)}) %all-gather.6.cloned.1.call-update) | async-done | bytes 1048592 | tf_op jit(solution)/shard_map/all_gather | solution.py:54
  75.3 0.0 copy-done
  75.3 4.1 %fusion.15 = f32[256,64]{0,1:T(8,128)} fusion(f32[16,256,64]{2,1,0:T(8,128)} %all-gather.6.cloned.1.call-done, bf16[32,16,8,256]{3,2,1,0:T(8,128)(2,1)S(1)} %bitcast.54), kind=kOutput, calls=%fused_computation.13 | convolution fusion | flops 805306368 | bytes 3211264 | tf_op jit(solution)/shard_map/tnk,nkm->tm/dot_general | solution.py:13
  79.4 107.8 %all-gather.4.cloned.1.call-done = f32[56,256,64]{2,1,0:T(8,128)} async-done(((f32[56,16,64]{2,1,0:T(8,128)}), f32[56,256,64]{2,1,0:T(8,128)}) %all-gather.4.cloned.1.call-update) | async-done | bytes 3670032 | tf_op jit(solution)/shard_map/all_gather | solution.py:53
  187.3 0.0 copy-start.4
  187.3 0.0 copy-start.5
  187.3 0.0 copy-start.6
  187.3 12.0 %fusion.12 = f32[256,64]{0,1:T(8,128)} fusion(f32[56,256,64]{2,1,0:T(8,128)} %all-gather.4.cloned.1.call-done, bf16[32,56,8,256]{3,2,1,0:T(8,128)(2,1)} %bitcast.52), kind=kOutput, calls=%fused_computation.12 | convolution fusion | flops 2818572288 | bytes 11075584 | tf_op jit(solution)/shard_map/tnk,nkm->tm/dot_general | solution.py:13
  199.3 0.0 all-reduce.3.cloned.1.call-update
  199.3 0.0 copy-done.4
  199.3 0.0 copy-done.5
  199.3 16.3 %all-reduce.3.cloned.1.call-done = (f32[256,64]{0,1:T(8,128)}, f32[256,64]{0,1:T(8,128)}) async-done(((f32[256,64]{0,1:T(8,128)}, f32[256,64]{0,1:T(8,128)}), (f32[256,64]{0,1:T(8,128)}, f32[256,64]{0,1:T(8,128)})) %all-reduce.3.cloned.1.call-update) | async-done | bytes 131088 | tf_op jit(solution)/shard_map/psum | solution.py:55
  215.6 0.9 bitcast_reduce_fusion
  216.5 0.0 copy-start.3
  216.5 0.1 convolution_divide_fusion
  216.7 40.9 %all-gather = f32[16,2,4]{2,1,0:T(2,128)S(1)} all-gather(f32[1,2,4]{2,1,0:T(2,128)S(1)} %subtract_bitcast_fusion), channel_id=1, replica_groups=mesh['groups'=1,'train'=16,'tensor'=2] {'train'}, dimensions={0}, use_global_device_ids=true | all-gather | bytes 544 | tf_op jit(solution)/shard_map/all_gather | solution.py:67
  257.6 0.0 copy-done.6
  257.6 0.8 fusion.25
  258.4 0.0 copy-done.3
  (7 shorter events, 0.1 us)
Async XLA Ops:
  7.2 3.6 %copy-start.1 = (bf16[14336,64]{0,1:T(8,128)(2,1)S(1)}, bf16[14336,64]{0,1:T(8,128)(2,1)}, u32[]{:S(2)}) copy-start(bf16[14336,64]{0,1:T(8,128)(2,1)} %param.17) | copy-start | bytes 5505028
  7.2 68.2 %all-gather.6.cloned.1.call-start = ((), (), s32[]{:S(2)}) async-start(), calls=%async_computation.1 | async-start | bytes 2228224 | tf_op jit(solution)/shard_map/all_gather | solution.py:54
  8.5 3.4 %copy-start.2 = (bf16[16,14336]{1,0:T(8,128)(2,1)S(1)}, bf16[16,14336]{1,0:T(8,128)(2,1)}, u32[]{:S(2)}) copy-start(bf16[16,14336]{1,0:T(8,128)(2,1)} %param.13) | copy-start | bytes 1376260
  10.7 176.5 %all-gather.4.cloned.1.call-start = ((), (), s32[]{:S(2)}) async-start(), calls=%async_computation | async-start | bytes 7798784 | tf_op jit(solution)/shard_map/all_gather | solution.py:53
  11.9 63.5 %copy-start = (bf16[256,4096]{1,0:T(8,128)(2,1)S(1)}, bf16[256,4096]{1,0:T(8,128)(2,1)}, u32[]{:S(2)}) copy-start(bf16[256,4096]{1,0:T(8,128)(2,1)} %param.12) | copy-start | bytes 6291460
  14.6 201.1 %all-reduce.3.cloned.1.call-start = ((), (), s32[]{:S(2)}) async-start(), calls=%async_computation.2 | async-start | bytes 262144 | tf_op jit(solution)/shard_map/psum | solution.py:55
  187.3 12.0 %copy-start.4 = (s32[256]{0:T(256)S(1)}, s32[256]{0:T(256)}, u32[]{:S(2)}) copy-start(s32[256]{0:T(256)} %param.19) | copy-start | bytes 3076
  187.3 12.0 %copy-start.5 = (s32[4]{0:T(128)S(1)}, s32[4]{0:T(128)}, u32[]{:S(2)}) copy-start(s32[4]{0:T(128)} %param.20) | copy-start | bytes 52
  187.3 70.3 %copy-start.6 = (s32[32]{0:T(128)S(1)}, s32[32]{0:T(128)}, u32[]{:S(2)}) copy-start(s32[32]{0:T(128)} %param.21) | copy-start | bytes 388
  216.5 41.8 %copy-start.3 = (f32[256,4]{0,1:T(4,128)}, f32[256,4]{0,1:T(4,128)S(1)}, u32[]{:S(2)}) copy-start(f32[256,4]{0,1:T(4,128)S(1)} %constant_dynamic-slice_fusion) | copy-start | bytes 12292
Sparse Core Ops, SparseCore 0:
  10.8 64.4 all-gather.5
  78.0 109.1 all-gather.3
  199.4 16.1 all-reduce.2
where the time goes:
time: 265 us
  waiting for transfers between devices  185 us (70%)
  blocking collectives  40.9 us (15%)
  matrix products  21.8 us (8%)
  between operations  13.9 us (5%)
  other arithmetic  3.25 us (1%)
    all_gather x1, waiting for transfers between devices, shards(): lax.all_gather(folded_in, 'train', axis=1, tiled=True)  108 us
    all_gather x1, waiting for transfers between devices, shards(): lax.all_gather(folded_out, 'train', axis=1, tiled=True)  60.7 us
    all_gather x1, blocking collectives, shards(): every_slot = lax.all_gather(slot_values, 'train', axis=0, tiled=True)  40.9 us
    psum x1, waiting for transfers between devices, shards(): proj_in, proj_out = lax.psum((proj_in, proj_out), 'tensor')  16.3 us
    dot_general x2, matrix products, apply_fn(): jnp.einsum('tnk,nkm->tm', token_rows, fetched, precision=lax.Precision.HI...  16.1 us
  transfers between devices with their start and end apart: 3, of which 3 were waited for; matrix products, arithmetic and copies ran while one was open for 3% of the time, Pallas kernels for 0%

commit v1 on v0

--- a/solution.py
+++ b/solution.py
@@ -1,7 +1,13 @@
+import functools
+
 import jax
 import jax.numpy as jnp
 from jax import lax
+from jax.experimental import pallas as pl
+from jax.experimental.pallas import tpu as pltpu
 from jax.sharding import PartitionSpec as P
+
+MESH = pl.DeviceIdType.MESH
 
 BLOCK_IN = 256
 BLOCK_OUT = 256
@@ -72,9 +78,350 @@
     return (scores, pair_scores)
 
 
+SHARE = 16
+DEPTH = 4
+CHUNKS = 4
+
+
+def fused_kernel(
+    act_hbm,
+    grad_hbm,
+    basis_in_hbm,
+    basis_out_hbm,
+    eigen_in_hbm,
+    eigen_out_hbm,
+    query_in_hbm,
+    query_out_hbm,
+    ids_ref,
+    lengths_ref,
+    pair_ids_ref,
+    scores_ref,
+    pairs_ref,
+    rows,
+    basis,
+    eigen,
+    query,
+    fold,
+    proj,
+    other,
+    slots,
+    local_sem,
+    send_sem,
+    z_sem,
+    x_sem,
+    y_sem,
+    xd_sem,
+    yd_sem,
+    proj_sem,
+    slot_send,
+    slot_recv,
+):
+    me = lax.axis_index("train")
+    core = lax.axis_index("tensor")
+    x, y, z = lax.rem(me, 2), lax.rem(me // 2, 2), me // 4
+    x_side = me + 1 - 2 * x
+    y_side = me + 2 - 4 * y
+    corner = me + 3 - 2 * x - 4 * y
+    partner = 1 - core
+    hidden = act_hbm.shape[1]
+    total = rows.shape[1]
+    blocks_in = hidden // BLOCK_IN
+    blocks = total // BLOCK_IN
+    per_chunk = blocks // CHUNKS
+    half = CHUNKS // 2
+
+    barrier = pltpu.get_barrier_semaphore()
+    for step in range(1, SHARE):
+        pl.semaphore_signal(
+            barrier, inc=1, device_id={"train": lax.rem(me + step, SHARE)}, device_id_type=MESH
+        )
+    pl.semaphore_signal(barrier, inc=1, device_id={"tensor": partner}, device_id_type=MESH)
+
+    first, second = pl.ds(0, hidden), pl.ds(hidden, total - hidden)
+    loads = []
+    pairs = [
+        (basis_in_hbm, basis.at[:, first]),
+        (basis_out_hbm, basis.at[:, second]),
+        (eigen_in_hbm, eigen.at[:, first]),
+        (eigen_out_hbm, eigen.at[:, second]),
+        (query_in_hbm, query.at[pl.ds(0, 64), first]),
+        (query_out_hbm, query.at[pl.ds(0, 64), second]),
+        (query_in_hbm, query.at[pl.ds(64, 64), first]),
+        (query_out_hbm, query.at[pl.ds(64, 64), second]),
+        (act_hbm, rows.at[:, first]),
+        (grad_hbm, rows.at[:, second]),
+    ]
+    for i, (a, b) in enumerate(pairs):
+        loads.append(pltpu.make_async_copy(a, b, local_sem.at[i]))
+    for load in loads[:8]:
+        load.start()
+    for load in loads[:8]:
+        load.wait()
+    for load in loads[8:]:
+        load.start()
+
+    low_lanes = lax.broadcasted_iota(jnp.int32, (16, 128), 1) >= 64
+
+    def fold_block(b, carry):
+        cols = pl.ds(pl.multiple_of(b * BLOCK_IN, BLOCK_IN), BLOCK_IN)
+        scaled = basis[:, cols].astype(jnp.float32) * (1.0 / eigen[:, cols])
+        high = scaled.astype(jnp.bfloat16)
+        low = (scaled - high.astype(jnp.float32)).astype(jnp.bfloat16)
+        weights = query[:, cols]
+        dims = (((1,), (1,)), ((), ()))
+        both = lax.dot_general(
+            jnp.concatenate([high, low], axis=0), weights, dims, preferred_element_type=jnp.float32
+        )
+        folded = both[:16] + both[16:]
+        top = folded.astype(jnp.bfloat16).astype(jnp.float32)
+        fold[me, b] = jnp.where(low_lanes, folded - top, top).astype(jnp.bfloat16)
+        return carry
+
+    pending = []
+
+    def copy_of(origin, chunk, index, sem, target):
+        ref = fold.at[origin, pl.ds(chunk * per_chunk, per_chunk)]
+        return pltpu.make_async_remote_copy(
+            src_ref=ref,
+            dst_ref=ref,
+            send_sem=send_sem.at[index],
+            recv_sem=sem,
+            device_id={"train": target},
+            device_id_type=MESH,
+        )
+
+    def send(when, origin, chunk, sem, target):
+        copy = copy_of(origin, chunk, len(pending), sem, target)
+        pending.append(((when,), chunk))
+        copy.start()
+
+    def send_if(when, cond, origin, chunk, sem, target):
+        copy = copy_of(origin, chunk, len(pending), sem, target)
+        pending.append(((when, cond), chunk))
+
+        @pl.when(cond)
+        def _():
+            copy.start()
+
+    def arrived(origin, chunk, sem):
+        copy_of(origin, chunk, 0, sem, x_side).wait_recv()
+
+    always = z >= 0
+    up, down = z < DEPTH - 1, z > 0
+
+    for chunk in range(CHUNKS):
+        lax.fori_loop(chunk * per_chunk, (chunk + 1) * per_chunk, fold_block, 0, unroll=6)
+        if chunk == 0:
+            pl.semaphore_wait(barrier, SHARE)
+        send_if(always, up, me, chunk, z_sem.at[0, 0, chunk], me + 4)
+        send_if(always, down, me, chunk, z_sem.at[1, 0, chunk], me - 4)
+        send(always, me, chunk, x_sem.at[z, chunk], x_side)
+        send(always, me, chunk, y_sem.at[z, chunk], y_side)
+
+    def column(step):
+        for chunk in range(CHUNKS):
+            for way, shift in ((0, -step), (1, step)):
+                when = z + shift >= 0 if shift < 0 else z + shift < DEPTH
+
+                @pl.when(when)
+                def _():
+                    origin = me + 4 * shift
+                    arrived(origin, chunk, z_sem.at[way, step - 1, chunk])
+                    if step < DEPTH - 1:
+                        cond, target = (up, me + 4) if way == 0 else (down, me - 4)
+                        send_if(when, cond, origin, chunk, z_sem.at[way, step, chunk], target)
+                    send(when, origin, chunk, x_sem.at[z + shift, chunk], x_side)
+                    send(when, origin, chunk, y_sem.at[z + shift, chunk], y_side)
+
+    def across(step):
+        shifts = (0,) if step == 0 else (-step, step)
+        for chunk in range(half):
+            for shift in shifts:
+                when = z + shift >= 0 if shift < 0 else z + shift < DEPTH
+
+                @pl.when(when)
+                def _():
+                    level = z + shift
+                    origin = x_side + 4 * shift
+                    arrived(origin, chunk, x_sem.at[level, chunk])
+                    send(when, origin, chunk, yd_sem.at[level, chunk], y_side)
+                    origin = y_side + 4 * shift
+                    arrived(origin, half + chunk, y_sem.at[level, half + chunk])
+                    send(when, origin, half + chunk, xd_sem.at[level, chunk], x_side)
+
+    column(1)
+    across(0)
+    column(2)
+    across(1)
+    column(3)
+    across(2)
+    across(3)
+
+    for load in loads[8:]:
+        load.wait()
+    for level in range(DEPTH):
+        shift = 4 * (level - z)
+        for chunk in range(half):
+            arrived(x_side + shift, half + chunk, x_sem.at[level, half + chunk])
+            arrived(y_side + shift, chunk, y_sem.at[level, chunk])
+            arrived(corner + shift, chunk, yd_sem.at[level, chunk])
+            arrived(corner + shift, half + chunk, xd_sem.at[level, chunk])
+
+    def apply_block(b, acc):
+        cols = pl.ds(pl.multiple_of(b * BLOCK_IN, BLOCK_IN), BLOCK_IN)
+        weights = fold[:, b].reshape(BLOCK_IN, 128)
+        return acc + jnp.dot(rows[:, cols], weights, preferred_element_type=jnp.float32)
+
+    zero = jnp.zeros((rows.shape[0], 128), jnp.float32)
+    for side, (start, stop) in enumerate(((0, blocks_in), (blocks_in, blocks))):
+        acc = lax.fori_loop(start, stop, apply_block, zero, unroll=8)
+        turned = acc.T
+        summed = turned[:64] + turned[64:]
+        proj[0, side] = summed[:32]
+        proj[1, side] = summed[32:]
+    swap = pltpu.make_async_remote_copy(
+        src_ref=proj.at[partner],
+        dst_ref=other,
+        send_sem=proj_sem.at[0],
+        recv_sem=proj_sem.at[1],
+        device_id={"tensor": partner},
+        device_id_type=MESH,
+    )
+    swap.start()
+
+    tokens = rows.shape[0]
+    own_ids = ids_ref[...] - me * 4
+    signs = []
+    for slot in range(2):
+        weight = jnp.zeros((1, tokens), jnp.float32)
+        for k, sign in ((2 * slot, 1.0), (2 * slot + 1, -1.0)):
+            count = jnp.full((1, tokens), lengths_ref[k], jnp.int32).astype(jnp.float32)
+            weight = weight + jnp.where(own_ids == k, sign / count, 0.0)
+        signs.append(weight)
+
+    swap.wait()
+    full = proj[core] + other[...]
+    scores = (full[0] * full[1]).reshape(4, RANK, tokens).sum(axis=1)
+    scores_ref[...] = scores
+    parts = [
+        jnp.broadcast_to(jnp.sum(scores * weight, axis=1, keepdims=True), (4, 128))
+        for weight in signs
+    ]
+    slots[me] = jnp.concatenate(parts, axis=0)
+
+    def slot_copy(step):
+        target = lax.rem(me + step, SHARE)
+        return pltpu.make_async_remote_copy(
+            src_ref=slots.at[me],
+            dst_ref=slots.at[me],
+            send_sem=slot_send.at[step],
+            recv_sem=slot_recv.at[step],
+            device_id={"train": target},
+            device_id_type=MESH,
+        )
+
+    for step in range(1, SHARE):
+        slot_copy(step).start()
+    for index, (conds, chunk) in enumerate(pending):
+
+        @pl.when(functools.reduce(jnp.logical_and, conds))
+        def _():
+            copy_of(me, chunk, index, x_sem.at[0, 0], x_side).wait_send()
+
+    for step in range(1, SHARE):
+        origin = lax.rem(me + SHARE - step, SHARE)
+        pltpu.make_async_remote_copy(
+            src_ref=slots.at[origin],
+            dst_ref=slots.at[origin],
+            send_sem=slot_send.at[step],
+            recv_sem=slot_recv.at[step],
+            device_id={"train": origin},
+            device_id_type=MESH,
+        ).wait_recv()
+        slot_copy(step).wait_send()
+
+    row = lax.broadcasted_iota(jnp.int32, (4, 128), 0)
+    lane = lax.broadcasted_iota(jnp.int32, (4, 128), 1)
+    for own in range(2):
+        value = jnp.zeros((4, 128), jnp.float32)
+        for k in range(2 * SHARE):
+            same = jnp.full((4, 128), pair_ids_ref[k], jnp.int32) == me * 2 + own
+            value = value + jnp.where(same, slots[k // 2, 4 * (k % 2) : 4 * (k % 2) + 4], 0.0)
+        line = jnp.sum(jnp.where(row == lane, value, 0.0), axis=0, keepdims=True)
+        pairs_ref[own : own + 1] = line[:, :4]
+
+
+def fused(
+    activations,
+    out_grads,
+    basis_in,
+    basis_out,
+    eigen_in,
+    eigen_out,
+    query_in,
+    query_out,
+    response_ids,
+    lengths,
+    pair_ids,
+):
+    tokens, hidden = activations.shape
+    total = hidden + out_grads.shape[1]
+    blocks = total // BLOCK_IN
+    share = basis_in.shape[0]
+    vmem = pl.BlockSpec(memory_space=pltpu.VMEM)
+    smem = pl.BlockSpec(memory_space=pltpu.SMEM)
+    scores, pair_scores = pl.pallas_call(
+        fused_kernel,
+        out_shape=(
+            jax.ShapeDtypeStruct((4, tokens), jnp.float32),
+            jax.ShapeDtypeStruct((2, 4), jnp.float32),
+        ),
+        in_specs=[pl.BlockSpec(memory_space=pl.ANY)] * 8 + [vmem, smem, smem],
+        out_specs=(vmem, vmem),
+        scratch_shapes=[
+            pltpu.VMEM((tokens, total), jnp.bfloat16),
+            pltpu.VMEM((share, total), jnp.bfloat16),
+            pltpu.VMEM((1, total), jnp.float32),
+            pltpu.VMEM((128, total), jnp.bfloat16),
+            pltpu.VMEM((SHARE, blocks, share, 128), jnp.bfloat16),
+            pltpu.VMEM((2, 2, 32, tokens), jnp.float32),
+            pltpu.VMEM((2, 32, tokens), jnp.float32),
+            pltpu.VMEM((SHARE, 8, 128), jnp.float32),
+            pltpu.SemaphoreType.DMA((10,)),
+            pltpu.SemaphoreType.DMA((40 * CHUNKS,)),
+            pltpu.SemaphoreType.DMA((2, DEPTH - 1, CHUNKS)),
+            pltpu.SemaphoreType.DMA((DEPTH, CHUNKS)),
+            pltpu.SemaphoreType.DMA((DEPTH, CHUNKS)),
+            pltpu.SemaphoreType.DMA((DEPTH, CHUNKS // 2)),
+            pltpu.SemaphoreType.DMA((DEPTH, CHUNKS // 2)),
+            pltpu.SemaphoreType.DMA((2,)),
+            pltpu.SemaphoreType.DMA((SHARE,)),
+            pltpu.SemaphoreType.DMA((SHARE,)),
+        ],
+        compiler_params=pltpu.CompilerParams(
+            collective_id=0, has_side_effects=True, vmem_limit_bytes=48 * 1024 * 1024
+        ),
+    )(
+        activations,
+        out_grads,
+        basis_in,
+        basis_out,
+        eigen_in.reshape(1, -1),
+        eigen_out.reshape(1, -1),
+        query_in.T,
+        query_out.T,
+        response_ids.reshape(1, -1),
+        lengths,
+        pair_ids,
+    )
+    return scores.T, pair_scores
+
+
 def solution(mesh):
+    sizes = (mesh.shape["groups"], mesh.shape["train"], mesh.shape["tensor"])
+    body = fused if sizes == (1, 16, 2) else shards
     return jax.shard_map(
-        shards,
+        body,
         mesh=mesh,
         in_specs=(
             P(("groups", "train"), "tensor"),

time: 265 us -> 69.6 us (0.26)
  waiting for transfers between devices: 185 us -> 0 us
  Pallas kernels: 0 us -> 57.8 us
  blocking collectives: 40.9 us -> 0 us
  matrix products: 21.8 us -> 0 us
  between operations: 13.9 us -> 0.66 us
  local copies, waits for them, and re-layouts: 0.1 us -> 10.7 us
  other arithmetic: 3.25 us -> 0 us
    all_gather x2 -> x0, waiting for transfers between devices: 169 us -> none  [the longest x1 108 us: shards(): lax.all_gather(folded_in, 'train', axis=1, tiled=True)]
    pallas_call x0 -> x1, Pallas kernels: none -> 57.8 us  [fused(): pl.pallas_call(fused_kernel, out_shape=(jax.ShapeDtypeStruct((4, tokens),...]
    all_gather x1 -> x0, blocking collectives: 40.9 us -> none  [shards(): every_slot = lax.all_gather(slot_values, 'train', axis=0, tiled=True)]
    dot_general x6 -> x0, matrix products: 21.8 us -> none  [the longest x2 16.1 us: apply_fn(): jnp.einsum('tnk,nkm->tm', token_rows, fetched, precision=lax.Precision.HI...]
    psum x1 -> x0, waiting for transfers between devices: 16.3 us -> none  [shards(): proj_in, proj_out = lax.psum((proj_in, proj_out), 'tensor')]
    unnamed x14 -> x22, local copies, waits for them, and re-layouts: 0.03 us -> 10.7 us
  transfers between devices with their start and end apart: 3 -> 0, of which waited for: 3 -> 0; matrix products, arithmetic and copies ran while one was open for 3% -> 0% of each run, Pallas kernels for 0% -> 0%
where the time goes in v1:
time: 69.6 us; the launch traced here: 69.2 us
  Pallas kernels  57.8 us (83%)
  local copies, waits for them, and re-layouts  10.7 us (15%)
    pallas_call x1, Pallas kernels, fused(): pl.pallas_call(fused_kernel, out_shape=(jax.ShapeDtypeStruct((4, tokens),...  57.8 us
    unnamed x22, local copies, waits for them, and re-layouts  10.7 us

profile of v1, /device:TPU:0, one launch (start us, length us, event | category | flops | bytes accessed | tf_op | source)
XLA Modules:
  0.0 69.2 jit_solution(1399809930281482728)
XLA Ops:
  0.6 0.0 copy-start
  0.6 1.6 %copy-done = bf16[256,4096]{1,0:T(8,128)(2,1)S(1)} copy-done((bf16[256,4096]{1,0:T(8,128)(2,1)S(1)}, bf16[256,4096]{1,0:T(8,128)(2,1)}, u32[]{:S(2)}) %copy-start) | copy-done | bytes 2097176
  2.2 0.0 copy-start.1
  2.2 1.5 %copy-done.1 = bf16[14336,64]{0,1:T(8,128)(2,1)S(1)} copy-done((bf16[14336,64]{0,1:T(8,128)(2,1)S(1)}, bf16[14336,64]{0,1:T(8,128)(2,1)}, u32[]{:S(2)}) %copy-start.1) | copy-done | bytes 1835032
  3.7 0.0 copy-start.2
  3.7 1.0 %copy-done.2 = bf16[4096,64]{0,1:T(8,128)(2,1)S(1)} copy-done((bf16[4096,64]{0,1:T(8,128)(2,1)S(1)}, bf16[4096,64]{0,1:T(8,128)(2,1)}, u32[]{:S(2)}) %copy-start.2) | copy-done | bytes 524312
  4.8 0.0 copy-start.3
  4.8 1.0 %copy-done.3 = bf16[16,14336]{1,0:T(8,128)(2,1)S(1)} copy-done((bf16[16,14336]{1,0:T(8,128)(2,1)S(1)}, bf16[16,14336]{1,0:T(8,128)(2,1)}, u32[]{:S(2)}) %copy-start.3) | copy-done | bytes 458776
  5.8 0.0 copy-start.4
  5.8 0.9 %copy-done.4 = bf16[16,4096]{1,0:T(8,128)(2,1)S(1)} copy-done((bf16[16,4096]{1,0:T(8,128)(2,1)S(1)}, bf16[16,4096]{1,0:T(8,128)(2,1)}, u32[]{:S(2)}) %copy-start.4) | copy-done | bytes 131096
  6.7 0.0 copy-start.5
  6.7 0.8 %copy-done.5 = f32[14336]{0:T(1024)S(1)} copy-done((f32[14336]{0:T(1024)S(1)}, f32[14336]{0:T(1024)}, u32[]{:S(2)}) %copy-start.5) | copy-done | bytes 57368
  7.5 0.0 copy-start.6
  7.5 0.7 %copy-done.6 = f32[4096]{0:T(1024)S(1)} copy-done((f32[4096]{0:T(1024)S(1)}, f32[4096]{0:T(1024)}, u32[]{:S(2)}) %copy-start.6) | copy-done | bytes 16408
  8.2 0.0 copy-start.7
  8.2 0.7 copy-done.7
  8.9 0.0 copy-start.8
  8.9 0.7 copy-done.8
  9.6 0.0 copy-start.9
  9.6 0.7 copy-done.9
  10.2 57.8 %shard_map.122 = (f32[4,256]{1,0:T(4,128)S(1)}, f32[2,4]{1,0:T(2,128)S(1)}) custom-call(bf16[256,14336]{1,0:T(8,128)(2,1)} %act_hbm.1, bf16[256,4096]{1,0:T(8,128)(2,1)S(1)} %copy-done, bf16[16,14336]{1,0:T(8,128)(2,1)S(1)} %copy-done.3, bf16[16,4096]{1,0:T(8,128)(2,1)S(1)} %copy-done.4, f32[1,14336]{1,0:T(1,128)S(1)} %bitcast.8, f32[1,4096]{1,0:T(1,128)S(1)} %bitcast.9, ...), custom_call_target="tpu_custom_call" | custom-call | tf_op jit(solution)/shard_map/pallas_call | solution.py:373
  68.0 0.6 copy.15
  68.6 0.6 copy.16
Async XLA Ops:
  0.6 1.6 %copy-start = (bf16[256,4096]{1,0:T(8,128)(2,1)S(1)}, bf16[256,4096]{1,0:T(8,128)(2,1)}, u32[]{:S(2)}) copy-start(bf16[256,4096]{1,0:T(8,128)(2,1)} %grad_hbm.1) | copy-start | bytes 6291460
  2.2 1.5 %copy-start.1 = (bf16[14336,64]{0,1:T(8,128)(2,1)S(1)}, bf16[14336,64]{0,1:T(8,128)(2,1)}, u32[]{:S(2)}) copy-start(bf16[14336,64]{0,1:T(8,128)(2,1)} %param.17) | copy-start | bytes 5505028
  3.7 1.0 %copy-start.2 = (bf16[4096,64]{0,1:T(8,128)(2,1)S(1)}, bf16[4096,64]{0,1:T(8,128)(2,1)}, u32[]{:S(2)}) copy-start(bf16[4096,64]{0,1:T(8,128)(2,1)} %param.18) | copy-start | bytes 1572868
  4.8 1.0 %copy-start.3 = (bf16[16,14336]{1,0:T(8,128)(2,1)S(1)}, bf16[16,14336]{1,0:T(8,128)(2,1)}, u32[]{:S(2)}) copy-start(bf16[16,14336]{1,0:T(8,128)(2,1)} %basis_in_hbm.1) | copy-start | bytes 1376260
  5.8 0.9 %copy-start.4 = (bf16[16,4096]{1,0:T(8,128)(2,1)S(1)}, bf16[16,4096]{1,0:T(8,128)(2,1)}, u32[]{:S(2)}) copy-start(bf16[16,4096]{1,0:T(8,128)(2,1)} %basis_out_hbm.1) | copy-start | bytes 393220
  6.7 0.8 %copy-start.5 = (f32[14336]{0:T(1024)S(1)}, f32[14336]{0:T(1024)}, u32[]{:S(2)}) copy-start(f32[14336]{0:T(1024)} %param.15) | copy-start | bytes 172036
  7.5 0.7 %copy-start.6 = (f32[4096]{0:T(1024)S(1)}, f32[4096]{0:T(1024)}, u32[]{:S(2)}) copy-start(f32[4096]{0:T(1024)} %param.16) | copy-start | bytes 49156
  8.2 0.7 copy-start.7
  8.9 0.7 copy-start.8
  9.6 0.7 copy-start.9

commit v2 on v1

--- a/solution.py
+++ b/solution.py
@@ -80,7 +80,8 @@
 
 SHARE = 16
 DEPTH = 4
-CHUNKS = 4
+CHUNKS = 2
+GROUP = 2
 
 
 def fused_kernel(
@@ -102,6 +103,7 @@
     eigen,
     query,
     fold,
+    scales,
     proj,
     other,
     slots,
@@ -127,7 +129,9 @@
     total = rows.shape[1]
     blocks_in = hidden // BLOCK_IN
     blocks = total // BLOCK_IN
-    per_chunk = blocks // CHUNKS
+    half_blocks = blocks // 2
+    data = half_blocks // CHUNKS
+    per_chunk = data + 1
     half = CHUNKS // 2
 
     barrier = pltpu.get_barrier_semaphore()
@@ -160,22 +164,37 @@
     for load in loads[8:]:
         load.start()
 
-    low_lanes = lax.broadcasted_iota(jnp.int32, (16, 128), 1) >= 64
-
-    def fold_block(b, carry):
+    upper = lax.broadcasted_iota(jnp.int32, (16, 128), 1) >= 64
+    row_of = lax.broadcasted_iota(jnp.int32, (16, 128), 0)
+
+    def fold_block(b):
         cols = pl.ds(pl.multiple_of(b * BLOCK_IN, BLOCK_IN), BLOCK_IN)
         scaled = basis[:, cols].astype(jnp.float32) * (1.0 / eigen[:, cols])
         high = scaled.astype(jnp.bfloat16)
         low = (scaled - high.astype(jnp.float32)).astype(jnp.bfloat16)
-        weights = query[:, cols]
         dims = (((1,), (1,)), ((), ()))
         both = lax.dot_general(
-            jnp.concatenate([high, low], axis=0), weights, dims, preferred_element_type=jnp.float32
+            jnp.concatenate([high, low], axis=0),
+            query[:, cols],
+            dims,
+            preferred_element_type=jnp.float32,
         )
-        folded = both[:16] + both[16:]
-        top = folded.astype(jnp.bfloat16).astype(jnp.float32)
-        fold[me, b] = jnp.where(low_lanes, folded - top, top).astype(jnp.bfloat16)
-        return carry
+        return both[:16] + both[16:]
+
+    def fold_group(chunk, r, exponents):
+        values = []
+        for i in range(GROUP):
+            b = chunk * data + r * GROUP + i
+            values.append(jnp.where(upper, fold_block(b + half_blocks), fold_block(b)))
+        largest = functools.reduce(jnp.maximum, [jnp.abs(v) for v in values])
+        largest = jnp.maximum(jnp.max(largest, axis=0, keepdims=True), 1e-30)
+        exponent = jnp.floor(jnp.log2(largest)) - 14.0
+        inverse = jnp.exp2(-exponent)
+        for i, v in enumerate(values):
+            steps = jnp.clip(jnp.round(v * inverse), -32767.0, 32767.0)
+            tile = chunk * per_chunk + r * GROUP + i
+            fold[me, tile] = steps.astype(jnp.int32).astype(jnp.int16)
+        return jnp.where(row_of == r, exponent, exponents)
 
     pending = []
 
@@ -210,7 +229,14 @@
     up, down = z < DEPTH - 1, z > 0
 
     for chunk in range(CHUNKS):
-        lax.fori_loop(chunk * per_chunk, (chunk + 1) * per_chunk, fold_block, 0, unroll=6)
+        exponents = lax.fori_loop(
+            0,
+            data // GROUP,
+            functools.partial(fold_group, chunk),
+            jnp.zeros((16, 128), jnp.float32),
+            unroll=3,
+        )
+        fold[me, chunk * per_chunk + data] = exponents.astype(jnp.int32).astype(jnp.int16)
         if chunk == 0:
             pl.semaphore_wait(barrier, SHARE)
         send_if(always, up, me, chunk, z_sem.at[0, 0, chunk], me + 4)
@@ -267,14 +293,38 @@
             arrived(corner + shift, chunk, yd_sem.at[level, chunk])
             arrived(corner + shift, half + chunk, xd_sem.at[level, chunk])
 
-    def apply_block(b, acc):
-        cols = pl.ds(pl.multiple_of(b * BLOCK_IN, BLOCK_IN), BLOCK_IN)
-        weights = fold[:, b].reshape(BLOCK_IN, 128)
-        return acc + jnp.dot(rows[:, cols], weights, preferred_element_type=jnp.float32)
+    for chunk in range(CHUNKS):
+        for origin in range(SHARE):
+            held = fold[origin, chunk * per_chunk + data].astype(jnp.int32).astype(jnp.float32)
+            scales[chunk, origin] = jnp.exp2(held)
+
+    wide = lax.broadcasted_iota(jnp.int32, (BLOCK_IN, 128), 1) >= 64
+
+    def parts_of(folded):
+        top = folded.astype(jnp.bfloat16).astype(jnp.float32)
+        return jnp.where(wide, folded - top, top).astype(jnp.bfloat16)
+
+    def apply_pair(p, carry):
+        acc_one, acc_two = carry
+        chunk = p // data
+        group = lax.rem(p, data) // GROUP
+        steps = fold[:, p + chunk].astype(jnp.int32).astype(jnp.float32)
+        values = (steps * scales[chunk, :, pl.ds(group, 1), :]).reshape(BLOCK_IN, 128)
+        turned = pltpu.roll(values, 64, 1)
+        one = parts_of(jnp.where(wide, turned, values))
+        two = parts_of(jnp.where(wide, values, turned))
+        cols = pl.ds(pl.multiple_of(p * BLOCK_IN, BLOCK_IN), BLOCK_IN)
+        acc_one = acc_one + jnp.dot(rows[:, cols], one, preferred_element_type=jnp.float32)
+        cols = pl.ds(pl.multiple_of((p + half_blocks) * BLOCK_IN, BLOCK_IN), BLOCK_IN)
+        acc_two = acc_two + jnp.dot(rows[:, cols], two, preferred_element_type=jnp.float32)
+        return acc_one, acc_two
 
     zero = jnp.zeros((rows.shape[0], 128), jnp.float32)
-    for side, (start, stop) in enumerate(((0, blocks_in), (blocks_in, blocks))):
-        acc = lax.fori_loop(start, stop, apply_block, zero, unroll=8)
+    split = blocks_in - half_blocks
+    acc_one, acc_two = lax.fori_loop(0, split, apply_pair, (zero, zero), unroll=4)
+    sums_in = acc_one + acc_two
+    sums_in, sums_out = lax.fori_loop(split, half_blocks, apply_pair, (sums_in, zero), unroll=4)
+    for side, acc in enumerate((sums_in, sums_out)):
         turned = acc.T
         summed = turned[:64] + turned[64:]
         proj[0, side] = summed[:32]
@@ -383,7 +433,8 @@
             pltpu.VMEM((share, total), jnp.bfloat16),
             pltpu.VMEM((1, total), jnp.float32),
             pltpu.VMEM((128, total), jnp.bfloat16),
-            pltpu.VMEM((SHARE, blocks, share, 128), jnp.bfloat16),
+            pltpu.VMEM((SHARE, blocks // 2 + CHUNKS, share, 128), jnp.int16),
+            pltpu.VMEM((CHUNKS, SHARE, share, 128), jnp.float32),
             pltpu.VMEM((2, 2, 32, tokens), jnp.float32),
             pltpu.VMEM((2, 32, tokens), jnp.float32),
             pltpu.VMEM((SHARE, 8, 128), jnp.float32),
@@ -399,7 +450,7 @@
             pltpu.SemaphoreType.DMA((SHARE,)),
         ],
         compiler_params=pltpu.CompilerParams(
-            collective_id=0, has_side_effects=True, vmem_limit_bytes=48 * 1024 * 1024
+            collective_id=0, has_side_effects=True, vmem_limit_bytes=60 * 1024 * 1024
         ),
     )(
         activations,

time: 69.6 us -> 46.9 us (0.67)
  Pallas kernels: 57.8 us -> 43.6 us
  local copies, waits for them, and re-layouts: 10.7 us -> 2.48 us
    pallas_call x1, Pallas kernels: 57.8 us -> 43.6 us  [fused(): pl.pallas_call(fused_kernel, out_shape=(jax.ShapeDtypeStruct((4, tokens),...]
    unnamed x22 -> x2, local copies, waits for them, and re-layouts: 10.7 us -> 2.48 us
where the time goes in v2:
time: 46.9 us; the launch traced here: 46.7 us
  Pallas kernels  43.6 us (93%)
  local copies, waits for them, and re-layouts  2.48 us (5%)
  between operations  0.64 us (1%)
    pallas_call x1, Pallas kernels, fused(): pl.pallas_call(fused_kernel, out_shape=(jax.ShapeDtypeStruct((4, tokens),...  43.6 us
    unnamed x2, local copies, waits for them, and re-layouts  2.48 us

profile of v2, /device:TPU:0, one launch (start us, length us, event | category | flops | bytes accessed | tf_op | source)
XLA Modules:
  0.0 46.7 jit_solution(11835153839948166309)
XLA Ops:
  0.6 43.6 %shard_map.122 = (f32[4,256]{1,0:T(4,128)}, f32[2,4]{1,0:T(2,128)}) custom-call(bf16[256,14336]{1,0:T(8,128)(2,1)} %act_hbm.1, bf16[256,4096]{1,0:T(8,128)(2,1)} %grad_hbm.1, bf16[16,14336]{1,0:T(8,128)(2,1)} %basis_in_hbm.1, bf16[16,4096]{1,0:T(8,128)(2,1)} %basis_out_hbm.1, f32[1,14336]{1,0:T(1,128)} %bitcast.8, f32[1,4096]{1,0:T(1,128)} %bitcast.9, ...), custom_call_target="tpu_custom_call" | custom-call | tf_op jit(solution)/shard_map/pallas_call | solution.py:423
  44.2 1.3 %copy.15 = f32[256,4]{0,1:T(4,128)} copy(f32[256,4]{0,1:T(4,128)} %bitcast.10) | data formatting | bytes 8192
  45.5 1.2 %copy.16 = f32[2,4]{1,0:T(2,128)} copy(f32[2,4]{1,0:T(2,128)} %get-tuple-element.9) | data formatting | bytes 64

commit v3 on v2

--- a/solution.py
+++ b/solution.py
@@ -114,6 +114,7 @@
     y_sem,
     xd_sem,
     yd_sem,
+    zc_sem,
     proj_sem,
     slot_send,
     slot_recv,
@@ -275,23 +276,44 @@
                     arrived(origin, half + chunk, y_sem.at[level, half + chunk])
                     send(when, origin, half + chunk, xd_sem.at[level, chunk], x_side)
 
+    def corner_share():
+        for chunk in range(CHUNKS):
+            if chunk < half:
+                arrived(corner, chunk, yd_sem.at[z, chunk])
+            else:
+                arrived(corner, chunk, xd_sem.at[z, chunk - half])
+            send_if(always, up, corner, chunk, zc_sem.at[0, chunk], me + 4)
+            send_if(always, down, corner, chunk, zc_sem.at[1, chunk], me - 4)
+
     column(1)
     across(0)
     column(2)
-    across(1)
+    corner_share()
     column(3)
     across(2)
     across(3)
 
     for load in loads[8:]:
         load.wait()
-    for level in range(DEPTH):
-        shift = 4 * (level - z)
-        for chunk in range(half):
-            arrived(x_side + shift, half + chunk, x_sem.at[level, half + chunk])
-            arrived(y_side + shift, chunk, y_sem.at[level, chunk])
-            arrived(corner + shift, chunk, yd_sem.at[level, chunk])
-            arrived(corner + shift, half + chunk, xd_sem.at[level, chunk])
+    for chunk in range(half):
+        other_half = half + chunk
+        for shift in range(1 - DEPTH, DEPTH):
+            level = z + shift
+
+            @pl.when(jnp.logical_and(level >= 0, level < DEPTH))
+            def _():
+                lift = 4 * shift
+                arrived(x_side + lift, other_half, x_sem.at[level, other_half])
+                arrived(y_side + lift, chunk, y_sem.at[level, chunk])
+                if abs(shift) == 1:
+                    arrived(x_side + lift, chunk, x_sem.at[level, chunk])
+                    arrived(y_side + lift, other_half, y_sem.at[level, other_half])
+                    way = 0 if shift < 0 else 1
+                    arrived(corner + lift, chunk, zc_sem.at[way, chunk])
+                    arrived(corner + lift, other_half, zc_sem.at[way, other_half])
+                elif shift != 0:
+                    arrived(corner + lift, chunk, yd_sem.at[level, chunk])
+                    arrived(corner + lift, other_half, xd_sem.at[level, chunk])
 
     for chunk in range(CHUNKS):
         for origin in range(SHARE):
@@ -445,6 +467,7 @@
             pltpu.SemaphoreType.DMA((DEPTH, CHUNKS)),
             pltpu.SemaphoreType.DMA((DEPTH, CHUNKS // 2)),
             pltpu.SemaphoreType.DMA((DEPTH, CHUNKS // 2)),
+            pltpu.SemaphoreType.DMA((2, CHUNKS)),
             pltpu.SemaphoreType.DMA((2,)),
             pltpu.SemaphoreType.DMA((SHARE,)),
             pltpu.SemaphoreType.DMA((SHARE,)),

time: 46.9 us -> 45.3 us (0.966)
  Pallas kernels: 43.6 us -> 41.9 us
    pallas_call x1, Pallas kernels: 43.6 us -> 41.9 us  [fused(): pl.pallas_call(fused_kernel, out_shape=(jax.ShapeDtypeStruct((4, tokens),...]
where the time goes in v3:
time: 45.3 us; the launch traced here: 45.1 us
  Pallas kernels  41.9 us (92%)
  local copies, waits for them, and re-layouts  2.48 us (5%)
  between operations  0.64 us (1%)
    pallas_call x1, Pallas kernels, fused(): pl.pallas_call(fused_kernel, out_shape=(jax.ShapeDtypeStruct((4, tokens),...  41.9 us
    unnamed x2, local copies, waits for them, and re-layouts  2.48 us

profile of v3, /device:TPU:0, one launch (start us, length us, event | category | flops | bytes accessed | tf_op | source)
XLA Modules:
  0.0 45.1 jit_solution(11392723815279067271)
XLA Ops:
  0.6 41.9 %shard_map.122 = (f32[4,256]{1,0:T(4,128)}, f32[2,4]{1,0:T(2,128)}) custom-call(bf16[256,14336]{1,0:T(8,128)(2,1)} %act_hbm.1, bf16[256,4096]{1,0:T(8,128)(2,1)} %grad_hbm.1, bf16[16,14336]{1,0:T(8,128)(2,1)} %basis_in_hbm.1, bf16[16,4096]{1,0:T(8,128)(2,1)} %basis_out_hbm.1, f32[1,14336]{1,0:T(1,128)} %bitcast.8, f32[1,4096]{1,0:T(1,128)} %bitcast.9, ...), custom_call_target="tpu_custom_call" | custom-call | tf_op jit(solution)/shard_map/pallas_call | solution.py:445
  42.6 1.3 %copy.15 = f32[256,4]{0,1:T(4,128)} copy(f32[256,4]{0,1:T(4,128)} %bitcast.10) | data formatting | bytes 8192
  43.9 1.2 %copy.16 = f32[2,4]{1,0:T(2,128)} copy(f32[2,4]{1,0:T(2,128)} %get-tuple-element.9) | data formatting | bytes 64

commit v4 on v3

--- a/solution.py
+++ b/solution.py
@@ -343,9 +343,9 @@
 
     zero = jnp.zeros((rows.shape[0], 128), jnp.float32)
     split = blocks_in - half_blocks
-    acc_one, acc_two = lax.fori_loop(0, split, apply_pair, (zero, zero), unroll=4)
+    acc_one, acc_two = lax.fori_loop(0, split, apply_pair, (zero, zero), unroll=10)
     sums_in = acc_one + acc_two
-    sums_in, sums_out = lax.fori_loop(split, half_blocks, apply_pair, (sums_in, zero), unroll=4)
+    sums_in, sums_out = lax.fori_loop(split, half_blocks, apply_pair, (sums_in, zero), unroll=8)
     for side, acc in enumerate((sums_in, sums_out)):
         turned = acc.T
         summed = turned[:64] + turned[64:]

time: 45.3 us -> 44.2 us (0.976)
  Pallas kernels: 41.9 us -> 40.9 us
    pallas_call x1, Pallas kernels: 41.9 us -> 40.9 us  [fused(): pl.pallas_call(fused_kernel, out_shape=(jax.ShapeDtypeStruct((4, tokens),...]
where the time goes in v4:
time: 44.2 us; the launch traced here: 44 us
  Pallas kernels  40.9 us (93%)
  local copies, waits for them, and re-layouts  2.48 us (6%)
  between operations  0.64 us (1%)
    pallas_call x1, Pallas kernels, fused(): pl.pallas_call(fused_kernel, out_shape=(jax.ShapeDtypeStruct((4, tokens),...  40.9 us
    unnamed x2, local copies, waits for them, and re-layouts  2.48 us

profile of v4, /device:TPU:0, one launch (start us, length us, event | category | flops | bytes accessed | tf_op | source)
XLA Modules:
  0.0 44.0 jit_solution(5721649409524028057)
XLA Ops:
  0.6 40.9 %shard_map.122 = (f32[4,256]{1,0:T(4,128)}, f32[2,4]{1,0:T(2,128)}) custom-call(bf16[256,14336]{1,0:T(8,128)(2,1)} %act_hbm.1, bf16[256,4096]{1,0:T(8,128)(2,1)} %grad_hbm.1, bf16[16,14336]{1,0:T(8,128)(2,1)} %basis_in_hbm.1, bf16[16,4096]{1,0:T(8,128)(2,1)} %basis_out_hbm.1, f32[1,14336]{1,0:T(1,128)} %bitcast.8, f32[1,4096]{1,0:T(1,128)} %bitcast.9, ...), custom_call_target="tpu_custom_call" | custom-call | tf_op jit(solution)/shard_map/pallas_call | solution.py:445
  41.6 1.3 %copy.15 = f32[256,4]{0,1:T(4,128)} copy(f32[256,4]{0,1:T(4,128)} %bitcast.10) | data formatting | bytes 8192
  42.8 1.2 %copy.16 = f32[2,4]{1,0:T(2,128)} copy(f32[2,4]{1,0:T(2,128)} %get-tuple-element.9) | data formatting | bytes 64
